TPU v7x, 32 devices: a whole 2x2x4 slice. The times are simulated.
32 devices in a mesh: dp: 8 (over y, x, core), seq: 4 (over z).
Axes of the slice: x: 2, y: 2, z: 4, core: 2. Of those that a mesh axis runs over, the one named last changes fastest.
Arguments:
- activations: bfloat16 [16, 2048, 512], P('dp', 'seq'), may hold values from -6 to 6
- qkv_weight: bfloat16 [512, 1536], P('dp'), may hold values from -0.25 to 0.25
- attn_weight: bfloat16 [512, 512], P('dp'), may hold values from -1 to 1
- router_weight: bfloat16 [512, 8], P('dp'), may hold values from -0.125 to 0.125
- gain_one: bfloat16 [512], P('dp'), may hold values from 0.099609375 to 1.8984375
- gain_two: bfloat16 [512], P('dp'), may hold values from 0.099609375 to 1.8984375
- expert_in: bfloat16 [2048, 8, 512], P(('dp', 'seq')), may hold values from -0.25 to 0.25
- expert_out: bfloat16 [2048, 8, 512], P(('dp', 'seq')), may hold values from -0.125 to 0.125
- segments: int32 [16, 2048], P('dp', 'seq'), may hold values from 0 to 15, as said below
- task_ids: int32 [16, 2048], P('dp', 'seq'), may hold values from 0 to 15, as said below
- task_experts: int32 [16, 2], replicated, may hold values from 0 to 7, all different within a row
- out_grad: float32 [16, 2048, 512], P('dp', 'seq'), may hold values from -6 to 6
Outputs:
- outputs: bfloat16 [16, 2048, 512], P('dp', 'seq')
- input_grad: float32 [16, 2048, 512], P('dp', 'seq')
- qkv_grad: float32 [512, 1536], P('dp')
- attn_grad: float32 [512, 512], P('dp')
- router_grad: float32 [512, 8], P('dp')
- gain_one_grad: float32 [512], P('dp')
- gain_two_grad: float32 [512], P('dp')
- expert_in_grad: float32 [2048, 8, 512], P(('dp', 'seq'))
- expert_out_grad: float32 [2048, 8, 512], P(('dp', 'seq'))
Inputs may be any that keep to these rules, and one draw needn't show every extreme that they name: `segments`: segment numbers never fall along a pack and reach 15 in every draw; tokens attend only to tokens of their own pack with the same number; one pack of each index of dp is a single segment in every draw. `task_ids`: all tokens of a pack share one task; the 2 packs of one index of dp hold one or two tasks.
All inputs are finite; a program needn't handle non-finite values.
Results may differ from a plain program's by a relative error of at most 0.015.
Values may be sent and summed in bfloat16 or wider, within the bound.
A program may use at most 320 MiB of HBM per device.

v0:
```python
import functools

import jax
import jax.numpy as jnp
from jax import lax
from jax.experimental import pallas as pl
from jax.experimental.pallas import tpu as pltpu
from jax.sharding import PartitionSpec as P

HEAD = 64
LANES = 128
SEG_COL = HEAD
LSE_COL = HEAD + 16
SEGMENTS = 16
FAR = 1e9
LARGE = 62 << 20
NT = (((1,), (1,)), ((), ()))
TN = (((0,), (0,)), ((), ()))
MESH = pl.DeviceIdType.MESH
EXPERTS_AT = LANES - 1
TINY = 16
F32 = jnp.float32
LOW = jnp.bfloat16


def dot(a, b):
    return jnp.dot(a, b, preferred_element_type=F32)


def dot_nt(a, b):
    return lax.dot_general(a, b, NT, preferred_element_type=F32)


def dot_tn(a, b):
    return lax.dot_general(a, b, TN, preferred_element_type=F32)


def thirds(values):
    high = values.astype(LOW).astype(F32)
    rest = values - high
    mid = rest.astype(LOW).astype(F32)
    return high, mid, rest - mid


def lanes_of(shape):
    return lax.broadcasted_iota(jnp.int32, shape, len(shape) - 1)


def put_thirds(base, values, column):
    lane = lanes_of(base.shape)
    high, mid, last = thirds(values)
    base = jnp.where(lane == column, high, base)
    base = jnp.where(lane == column + 1, mid, base)
    return jnp.where(lane == column + 2, last, base)


def normalize(values):
    center = values - jnp.mean(values, axis=-1, keepdims=True)
    inverse = lax.rsqrt(jnp.mean(center * center, axis=-1, keepdims=True) + 1e-05)
    return center * inverse, inverse


def norm_backward(upstream, scaled, inverse, gain_vec):
    direct = upstream * gain_vec
    return inverse * (
        direct
        - jnp.mean(direct, axis=-1, keepdims=True)
        - scaled * jnp.mean(direct * scaled, axis=-1, keepdims=True)
    )


def cost(micros):
    return pl.CostEstimate(flops=int(micros * 1e7), bytes_accessed=1 << 10, transcendentals=0)


def whole(*shape):
    return pl.BlockSpec(shape, lambda *_: (0,) * len(shape))


def remote(source, target, send, receive, device):
    return pltpu.make_async_remote_copy(
        src_ref=source,
        dst_ref=target,
        send_sem=send,
        recv_sem=receive,
        device_id=device,
        device_id_type=MESH,
    )


def each(count, body):
    def step(i, carry):
        body(i)
        return carry

    lax.fori_loop(0, count, step, 0)


def layer_kernel(
    groups, planes, experts, te, acts, seg, up_in, qkv_in, attn_in, tiny_in, task, win_in, wout_in,
    tokens_out, grads_out, total_out, other_got, ga_got, gb_got, sel_out,
    x, segx, up, res, stage, both, other, near_all, attn_all, tiny_all, small, sel, task_all, task_s,
    qa, ka, va, att, attf, normed, gates, slot, dv, send, got_a, got_b, out, dx, far_value, far_dx,
    far_gate, att_grad, att_send, attn_acc, router_acc, gain_acc, rest_part, rest_got, gb, key_t,
    dq_acc, qkv_acc, first_acc, qkv_part, qkv_got, part, heard, summed, sums,
    sem_x, sem_seg, sem_on, sem_seg_on, sem_up, sem_up_on, sem_near, sem_attn, sem_tiny, sem_task,
    sem_phase, sem_a, sem_b, sem_ga, sem_gb, sem_att, sem_far, sem_sums, sem_out, sem_att_back,
    sem_rest, sem_back, sem_qkv, sem_in, sem_part, sem_total, home, local,
):
    me = lax.axis_index("dp")
    place = lax.axis_index("seq")
    core = lax.rem(me, 2)
    base = me - core
    partner = (base + 1 - core, place)
    peer = (me, place + 2 - 4 * (place // 2))
    band = 2 * (place // 2)
    mine = me * 2 + lax.rem(place, 2)
    count = 2 * groups
    piece, width = x.shape[1], x.shape[2]
    tokens = 2 * planes * piece
    half = tokens // 2
    chunks, _, _, rows, _ = send.shape
    chunk_rows = rows * experts
    heads = qa.shape[0]
    pairs = heads // 2
    near_width = heads * HEAD
    near_cols = near_all.shape[2]
    dense_rows = tiny_all.shape[2]
    stays = (place // 2) == core
    spot = core + 2 * lax.rem(place, 2)
    kinds = range(3)
    used = [0]

    def copy_here(source, target):
        copy = pltpu.make_async_copy(source, target, local.at[used[0]])
        used[0] += 1
        return copy

    def rows_of(b, size):
        return pl.ds(pl.multiple_of(b * size, size), size)

    kind_rows = both.shape[0] // 2
    load_up = copy_here(up_in, res)
    load_both = [
        copy_here(source, both.at[pl.ds(kind * kind_rows, source.shape[0])])
        for kind, source in enumerate((win_in, wout_in))
    ]
    load_up.start()
    for copy in load_both:
        copy.start()
    greet_all(groups, planes)

    def goes(d):
        return jnp.logical_not(stays & (d == spot))

    def token_copies(piece_of, target, sem, sem_on):
        def give_piece(d):
            to = (base + lax.rem(d, 2), 2 * core + d // 2)
            return remote(piece_of(d), target.at[place], sem.at[0, d], sem.at[1, place], to)

        at_home = copy_here(piece_of(spot), target.at[place])

        def start():
            def one(d):
                @pl.when(goes(d))
                def _():
                    give_piece(d).start()

            each(planes, one)

            @pl.when(stays)
            def _():
                at_home.start()

        def onward(k):
            return remote(target.at[k], target.at[planes + k], sem_on.at[0, k], sem_on.at[1, k], partner)

        def receive(k):
            home = stays & (k == place)

            @pl.when(home)
            def _():
                at_home.wait()

            @pl.when(jnp.logical_not(home))
            def _():
                remote(piece_of(0), target.at[k], sem.at[0, 0], sem.at[1, k], partner).wait_recv()

            onward(k).start()

        def finish():
            def one(d):
                @pl.when(goes(d))
                def _():
                    give_piece(d).wait_send()

                onward(d).wait_send()

            each(planes, one)

        return start, receive, lambda k: onward(k).wait_recv(), finish

    def seg_piece(d):
        return seg.at[:, rows_of(lax.rem(d, 2), piece)]

    x_start, x_receive, x_far, x_finish = token_copies(lambda d: acts.at[d], x, sem_x, sem_on)
    seg_start, seg_receive, seg_far, seg_finish = token_copies(seg_piece, segx, sem_seg, sem_seg_on)
    up_start, up_receive, up_far, up_finish = token_copies(
        lambda d: stage.at[d], up, sem_up, sem_up_on
    )

    def way_back(source, target, sem):
        def give_piece(k):
            to = (base + place // 2, k)
            return remote(source.at[k], target.at[spot], sem.at[0, k], sem.at[1, spot], to)

        at_home = copy_here(source.at[place], target.at[spot])

        def start(k):
            home = stays & (k == place)

            @pl.when(jnp.logical_not(home))
            def _():
                give_piece(k).start()

            @pl.when(home)
            def _():
                at_home.start()

        def end(d):
            @pl.when(jnp.logical_not(stays & (d == place)))
            def _():
                give_piece(d).wait_send()

            @pl.when(goes(d))
            def _():
                remote(source.at[0], target.at[d], sem.at[0, 0], sem.at[1, d], partner).wait_recv()

            @pl.when(stays & (d == place))
            def _():
                at_home.wait()

        return start, lambda: each(planes, end)

    out_start, out_end = way_back(stage, tokens_out, sem_out)
    in_start, in_end = way_back(up, grads_out, sem_in)

    def others(body):
        each(groups - 1, lambda i: body(lax.rem(me + 1 + i, groups)))

    def give(source, target, sem, i):
        return remote(source, target.at[me], sem.at[0, i], sem.at[1, me], (i, place))

    def taken(source, target, sem, i):
        return remote(source, target.at[i], sem.at[0, i], sem.at[1, i], (i, place))

    def near_part(i, kind):
        at = 2 * kind * near_width + lax.rem(i, 2) * near_width
        return qkv_in.at[:, pl.ds(pl.multiple_of(at, near_width), near_width)]

    def near_copy(i, kind, to, of):
        return remote(
            near_part(to, kind),
            near_all.at[of, :, pl.ds(kind * near_width, near_width)],
            sem_near.at[0, i, kind],
            sem_near.at[1, of, kind],
            (i, place),
        )

    def part_of(kind, c):
        at = kind * kind_rows + c * chunk_rows
        return pl.ds(at if isinstance(c, int) else pl.multiple_of(at, chunk_rows), chunk_rows)

    def phase_copy(kind, c):
        source = (win_in, wout_in)[kind].at[rows_of(c, chunk_rows)]
        target = other.at[part_of(kind, c)]
        return remote(source, target, sem_phase.at[0, kind, c], sem_phase.at[1, kind, c], peer)

    def sums_copy(kind, c):
        r = part_of(kind, c)
        return remote(
            sums.at[r], other_got.at[r], sem_sums.at[0, kind, c], sem_sums.at[1, kind, c], peer
        )

    def band_device(m):
        return (m // 2, band + lax.rem(m, 2))

    def band_copies(source, target, sem, home_sem):
        def give_part(c, m):
            to = band_device(m)
            return remote(source(c, m), target(c, mine), sem.at[c, 0, m], sem.at[c, 1, mine], to)

        def at_home(c):
            return pltpu.make_async_copy(source(c, mine), target(c, mine), home_sem.at[c])

        def run(body):
            each(count - 1, lambda i: body(lax.rem(mine + 1 + i, count)))

        def start(c):
            run(lambda m: give_part(c, m).start())
            at_home(c).start()

        def sent(c):
            run(lambda m: give_part(c, m).wait_send())

        def received(c):
            run(
                lambda m: remote(
                    source(c, m), target(c, m), sem.at[c, 0, m], sem.at[c, 1, m], band_device(m)
                ).wait_recv()
            )
            at_home(c).wait()

        return start, sent, received

    def by_chunk(source, target, sem, home_sem):
        return band_copies(
            lambda c, m: source.at[c, m], lambda c, m: target.at[c, m], sem, home_sem
        )

    a_start, a_sent, a_received = band_copies(
        lambda c, m: send.at[:, m], lambda c, m: got_a.at[:, m], sem_a, home.at[0]
    )
    b_start, b_sent, b_received = by_chunk(send, got_b, sem_b, home.at[1])
    ga_start, ga_sent, ga_received = by_chunk(got_a, ga_got, sem_ga, home.at[2])
    gb_start, gb_sent, gb_received = by_chunk(got_b, gb_got, sem_gb, home.at[3])

    def load_gb(c):
        return pltpu.make_async_copy(gb_got.at[c], send.at[c], home.at[4, c])

    x_start()
    seg_start()
    task_part = task.at[:, pl.ds(0, LANES)]
    others(lambda i: give(task_part, task_all, sem_task, i).start())
    others(lambda i: give(tiny_in, tiny_all, sem_tiny, i).start())

    def start_near(i):
        for kind in kinds:
            near_copy(i, kind, i, me).start()

    others(start_near)
    own_task = copy_here(task_part, task_all.at[me])
    own_dense = [
        copy_here(tiny_in, tiny_all.at[me]),
        copy_here(attn_in, attn_all.at[me]),
    ] + [
        copy_here(near_part(me, kind), near_all.at[me, :, pl.ds(kind * near_width, near_width)])
        for kind in kinds
    ]
    for copy in [own_task] + own_dense:
        copy.start()
    load_up.wait()
    stage[...] = res[...].astype(LOW)
    others(lambda i: taken(task_part, task_all, sem_task, i).wait_recv())
    own_task.wait()
    to_scalars = copy_here(task_all, task_s)
    to_scalars.start()
    to_scalars.wait()

    def expert_of(dp, z):
        at = z // 2 + dp - lax.rem(dp, 2)
        return te[lax.rem(dp, 2), task_s[at, lax.rem(z, 2), 0]]

    mine_id = expert_of(me, place)
    other_id = expert_of(partner[0], place)

    sel_row = lax.broadcasted_iota(jnp.int32, (rows, chunk_rows), 0)
    sel_col = lax.broadcasted_iota(jnp.int32, (rows, chunk_rows), 1)

    def fill_sel(m):
        dp, z = band_device(m)
        hit = sel_col == sel_row * experts + expert_of(dp, z)
        sel[m] = jnp.where(hit, 1.0, 0.0).astype(LOW)

    each(count, fill_sel)
    save_sel = copy_here(sel, sel_out)
    save_sel.start()

    def choose(source, c):
        choice = sel[...].reshape(count * rows, chunk_rows)
        for kind in range(2):
            values = dot(choice, source[part_of(kind, c), :])
            send[c, :, kind] = values.astype(LOW).reshape(count, rows, width)

    for copy in load_both:
        copy.wait()
    for c in range(chunks):
        choose(both, c)

    def end_near(i):
        for kind in kinds:
            near_copy(i, kind, i, i).wait_recv()

    others(end_near)
    others(lambda i: taken(tiny_in, tiny_all, sem_tiny, i).wait_recv())
    for copy in own_dense:
        copy.wait()
    eye = lax.broadcasted_iota(jnp.int32, (TINY, LANES), 0) == lanes_of((TINY, LANES))
    eye = jnp.where(eye, 1.0, 0.0).astype(LOW)

    def turn(i):
        small[rows_of(i, dense_rows), :] = dot_tn(tiny_all[i], eye)

    each(groups, turn)

    turned = small[...].T
    first_gain = turned[experts : experts + 1]
    second_gain = turned[experts + 1 : experts + 2]
    lane = lanes_of((piece, LANES))

    def project(k):
        scaled, _ = normalize(x[k].astype(F32))
        low = (scaled * first_gain).astype(LOW)
        values = dot(low, near_all[...].reshape(width, near_cols))
        segment = segx[k, pl.ds(lax.rem(place, 2), 1)].astype(F32)
        segment = jnp.broadcast_to(segment, (LANES, piece)).T
        same = (lane - SEG_COL).astype(F32) == segment
        in_seg = (lane >= SEG_COL) & (lane < SEG_COL + SEGMENTS)
        q_more = jnp.where(same, 1.0, 0.0)
        k_more = jnp.where(in_seg & jnp.logical_not(same), -FAR, 0.0)
        k_more = jnp.where((lane >= LSE_COL) & (lane < LSE_COL + 3), 1.0, k_more)
        v_more = jnp.where((lane >= HEAD) & (lane < HEAD + 3), 1.0, 0.0)
        r = rows_of(k, piece)

        def head(kind, h, more):
            at = kind * near_width + h // 2 * LANES
            values_of = values[:, at : at + LANES]
            if h % 2:
                values_of = pltpu.roll(values_of, HEAD, 1)
            return jnp.where(lane < HEAD, values_of, more)

        for h in range(heads):
            query = head(0, h, 0.0).astype(LOW).astype(F32) * HEAD**-0.5
            qa[h, r, :] = (query + q_more).astype(LOW)
            ka[h, r, :] = head(1, h, k_more).astype(LOW)
            va[h, r, :] = head(2, h, v_more).astype(LOW)

    def by_distance(k):
        return lax.bitwise_xor(place, jnp.int32(k))

    def arrive(k):
        x_receive(k)
        seg_receive(k)

    def start_phase(c):
        for kind in range(2):
            phase_copy(kind, c).start()

    for k in range(planes):
        arrive(by_distance(k))
        if k < planes // 2:
            project(by_distance(k))
    up_start()
    a_start(0)
    start_phase(0)
    others(lambda i: give(attn_in, attn_all, sem_attn, i).start())
    for k in range(planes // 2, planes):
        project(by_distance(k))

    def far_piece(k):
        x_far(k)
        seg_far(k)
        project(planes + k)

    each(planes, far_piece)

    block = min(512, half)

    def att_copy(p):
        return remote(att.at[p], attf.at[p], sem_att.at[0, p], sem_att.at[1, p], partner)

    for p in range(pairs):

        def attend(i):
            r = rows_of(i, block)
            parts = []
            for h in (2 * p, 2 * p + 1):
                query = qa[h, r, :]
                scores = dot_nt(query, ka[h])
                top = jnp.max(scores, axis=1, keepdims=True)
                probs = jnp.exp(scores - top).astype(LOW)
                mixed = dot(probs, va[h])
                total = mixed[:, HEAD : HEAD + 1]
                parts.append(mixed[:, :HEAD] / total)
                lse = top + jnp.log(total)
                qa[h, r, :] = put_thirds(query.astype(F32), -lse, LSE_COL).astype(LOW)
            att[p, r, :] = jnp.concatenate(parts, axis=1).astype(LOW)

        each(tokens // block, attend)
        att_copy(p).start()
        if p == 0 and chunks > 1:
            start_phase(1)

    def other_weights(c):
        for kind in range(2):
            phase_copy(kind, c).wait_recv()
        choose(other, c)
        b_start(c)

    for c in range(2, chunks):
        start_phase(c)
    for k in range(planes):
        up_receive(by_distance(k))
    for p in range(pairs):
        att_copy(p).wait_recv()
    others(lambda i: taken(attn_in, attn_all, sem_attn, i).wait_recv())

    def weight_rows(which):
        values = attn_all[pl.ds(which * (groups // 2), groups // 2)]
        return values.reshape(width // 2, width)

    def middle(b):
        @pl.when(b >= planes)
        def _():
            up_far(b - planes)

        r = rows_of(b, piece)
        f = rows_of(lax.rem(b + planes, 2 * planes), piece)
        residual = x[b].astype(F32)
        near_att = jnp.concatenate([att[p, r, :] for p in range(pairs)], axis=1)
        far_att = jnp.concatenate([attf[p, f, :] for p in range(pairs)], axis=1)
        residual += dot(near_att, weight_rows(core)) + dot(far_att, weight_rows(1 - core))

        @pl.when(b < planes)
        def _():
            res[b] = residual

        scaled, _ = normalize(residual)
        low = (scaled * second_gain).astype(LOW)
        normed[r, :] = low
        logits = dot(low, small[...].astype(LOW))
        of_mine = jnp.sum(jnp.where(lane == mine_id, logits, 0.0), axis=1, keepdims=True)
        of_other = jnp.sum(jnp.where(lane == other_id, logits, 0.0), axis=1, keepdims=True)
        top = jnp.maximum(of_mine, of_other)
        of_mine = jnp.exp(of_mine - top)
        of_other = jnp.exp(of_other - top)
        total = of_mine + of_other
        gate = of_mine / total
        gates[r, :] = jnp.where(lane == 0, gate, jnp.where(lane == 1, of_other / total, 0.0))
        slot[r, :] = (gate * up[b].astype(F32)).astype(LOW)

    each(2 * planes, middle)

    def add_up_others(c):
        b_sent(c)
        gb_received(c)
        load_gb(c).start()
        load_gb(c).wait()
        choice = sel[...].reshape(count * rows, chunk_rows)
        for kind in range(2):
            values = send[c, :, kind].reshape(count * rows, width)
            sums[part_of(kind, c), :] = dot_tn(choice, values).astype(LOW)
            sums_copy(kind, c).start()

    out[...] = jnp.zeros_like(out)
    dx[...] = jnp.zeros_like(dx)
    per = max(1, 256 // rows)

    def expert(weights, c):
        def tile(t):
            at = pl.ds(t * per, per)
            win = weights[c, at, 0].reshape(per * rows, width)
            wout = weights[c, at, 1].reshape(per * rows, width)
            pre = dot_nt(normed[...], win)
            hidden_grad = dot_nt(slot[...], wout)
            cdf = 0.5 * (1.0 + lax.erf(pre * 0.7071067811865476))
            slope = cdf + pre * jnp.exp(-0.5 * pre * pre) * 0.3989422804014327
            hidden = (pre * cdf).astype(LOW)
            pre_grad = (hidden_grad * slope).astype(LOW)
            out[...] += dot(hidden, wout)
            dx[...] += dot(pre_grad, win)
            weights[c, at, 0] = dot_tn(pre_grad, normed[...]).astype(LOW).reshape(per, rows, width)
            weights[c, at, 1] = dot_tn(hidden, slot[...]).astype(LOW).reshape(per, rows, width)

        each(count // per, tile)

    def second(c):
        b_received(c)
        expert(got_b, c)
        gb_start(c)

    a_sent(0)
    a_received(0)
    if chunks > 1:
        other_weights(0)
        expert(got_a, 0)
        other_weights(1)
        expert(got_a, 1)
        second(0)
        other_weights(2)
        expert(got_a, 2)
        second(1)
        other_weights(3)
        expert(got_a, 3)
        add_up_others(0)
        second(2)
        add_up_others(1)
        second(3)
    else:
        expert(got_a, 0)
        other_weights(0)
        second(0)

    step = half // 2
    step_lane = lanes_of((step, LANES))
    for at in range(0, tokens, step):
        r = pl.ds(at, step)
        value = out[r, :]
        upstream = up[pl.ds(at // piece, step // piece)].reshape(step, width).astype(F32)
        gate_grad = jnp.sum(value * upstream, axis=1, keepdims=True)
        value = value * gates[r, 0:1]
        if at < half:
            out[r, :] = value
            gates[r, :] = jnp.where(step_lane == 2, gate_grad, gates[r, :])
        else:
            t = pl.ds(at - half, step)
            other[t, :] = value.astype(LOW)
            both[t, :] = dx[r, :].astype(LOW)
            gates[r, :] = jnp.broadcast_to(gate_grad, (step, LANES))
    far_copies = [
        remote(other.at[pl.ds(0, half)], far_value, sem_far.at[0, 0], sem_far.at[1, 0], partner),
        remote(both.at[pl.ds(0, half)], far_dx, sem_far.at[0, 1], sem_far.at[1, 1], partner),
        remote(gates.at[pl.ds(half, half)], far_gate, sem_far.at[0, 2], sem_far.at[1, 2], partner),
    ]
    for copy in far_copies:
        copy.start()
    up_finish()

    res_grad = out.at[pl.ds(half, half)]
    attn_acc[...] = jnp.zeros_like(attn_acc)
    router_acc[...] = jnp.zeros_like(router_acc)
    gain_acc[...] = jnp.zeros_like(gain_acc)
    for copy in far_copies:
        copy.wait()


    def post(b):
        r = rows_of(b, piece)
        residual = res[b]
        upstream = up[b].astype(F32)
        stage[b] = (residual + out[r, :] + far_value[r, :].astype(F32)).astype(LOW)
        out_start(b)
        gate = gates[r, :]
        gate_mine, gate_other, grad_mine = gate[:, 0:1], gate[:, 1:2], gate[:, 2:3]
        grad_other = far_gate[r, 0:1]
        mean = gate_mine * grad_mine + gate_other * grad_other
        logit_grad = jnp.where(lane == mine_id, gate_mine * (grad_mine - mean), 0.0)
        logit_grad += jnp.where(lane == other_id, gate_other * (grad_other - mean), 0.0)
        normed_grad = dx[r, :] + far_dx[r, :].astype(F32)
        router = small[...].astype(LOW)
        for third in thirds(logit_grad):
            third = third.astype(LOW)
            router_acc[...] += dot_tn(normed[r, :], third)
            normed_grad += dot_nt(third, router)
        scaled, inverse = normalize(residual)
        gain_acc[...] += jnp.sum(normed_grad * scaled, axis=0, keepdims=True)
        residual_grad = upstream + norm_backward(normed_grad, scaled, inverse, second_gain)
        res_grad[r, :] = residual_grad
        low = residual_grad.astype(LOW)
        f = pl.ds(pl.multiple_of(half + b * piece, piece), piece)
        both_att = [att[p, r, :] for p in range(pairs)] + [attf[p, f, :] for p in range(pairs)]
        for i, values in enumerate(both_att):
            attn_acc[i * LANES : (i + 1) * LANES] += dot_tn(values, low)
        near_back = dot_nt(low, weight_rows(core)).astype(LOW)
        far_back = dot_nt(low, weight_rows(1 - core)).astype(LOW)
        for p in range(pairs):
            att_grad[p, r, :] = near_back[:, p * LANES : (p + 1) * LANES]
            att_send[p, r, :] = far_back[:, p * LANES : (p + 1) * LANES]

    each(planes, post)

    def att_back_copy(p):
        target = att_grad.at[p, pl.ds(half, half)]
        return remote(att_send.at[p], target, sem_att_back.at[0, p], sem_att_back.at[1, p], partner)

    for p in range(pairs):
        att_back_copy(p).start()
    own_rows = near_width // dense_rows
    turned = jnp.broadcast_to(gain_acc[...], (LANES, width)).T
    tail = jnp.where(lanes_of(turned.shape) == EXPERTS_AT, turned, router_acc[...]).astype(LOW)
    rest_part[:, :, width:] = tail.reshape(groups, dense_rows, LANES)
    for side in range(2):
        values = attn_acc[side * near_width : (side + 1) * near_width].astype(LOW)
        at = core if side == 0 else 1 - core
        rest_part[pl.ds(at * own_rows, own_rows), :, :width] = values.reshape(
            own_rows, dense_rows, width
        )

    def rest_copy(i):
        return give(rest_part.at[i], rest_got, sem_rest, i)

    others(lambda i: rest_copy(i).start())

    if chunks > 1:
        add_up_others(2)

    all_lane = lanes_of((tokens, LANES))
    for p in range(pairs):
        att_back_copy(p).wait_recv()
        halves = []
        for side in range(2):
            h = 2 * p + side
            pair_grad = att_grad[p].astype(F32)
            inner = pair_grad * att[p].astype(F32)
            if side == 1:
                pair_grad = pltpu.roll(pair_grad, HEAD, 1)
                inner = pltpu.roll(inner, HEAD, 1)
            delta = jnp.sum(jnp.where(all_lane < HEAD, inner, 0.0), axis=1, keepdims=True)
            pair_grad = jnp.where(all_lane < HEAD, pair_grad, 0.0)
            gb[...] = put_thirds(pair_grad, -delta, HEAD).astype(LOW)
            key_t[...] = ka[h].T[:HEAD]
            dq_acc[...] = jnp.zeros_like(dq_acc)
            dk_cols = pl.ds((pairs + p) * LANES + side * HEAD, HEAD)
            dv_cols = pl.ds(p * LANES + side * HEAD, HEAD)

            def keys(i):
                r = rows_of(i, block)
                weights = jnp.exp(dot_nt(ka[h, r, :], qa[h]))
                centered = dot_nt(va[h, r, :], gb[...])
                score_grad = (weights * centered).astype(LOW)
                dv[r, dv_cols] = dot(weights.astype(LOW), gb[...])[:, :HEAD].astype(LOW)
                slot[r, dk_cols] = dot(score_grad, qa[h])[:, :HEAD].astype(LOW)
                dq_acc[...] += dot(key_t[:, r], score_grad)

            each(tokens // block, keys)
            halves.append(dq_acc[...].T * HEAD**-0.5)
            if h == 0:
                add_up_others(chunks - 1)
                each(chunks, ga_start)
        slot[:, p * LANES : (p + 1) * LANES] = jnp.concatenate(halves, axis=1).astype(LOW)

    qkv_acc[...] = jnp.zeros_like(qkv_acc)
    first_acc[...] = jnp.zeros_like(first_acc)
    back_near = dx.at[pl.ds(half, half)]
    back_send = normed.at[pl.ds(0, half)]
    back_got = normed.at[pl.ds(half, half)]

    def project_back(b):
        r = rows_of(b, piece)
        values = jnp.concatenate([slot[r, :], dv[r, :]], axis=1)
        scaled, _ = normalize(x[b].astype(F32))
        back = dot_nt(values, near_all[...].reshape(width, near_cols))
        qkv_acc[...] += dot_tn((scaled * first_gain).astype(LOW), values)
        first_acc[...] += jnp.sum(back * scaled, axis=0, keepdims=True)
        return back

    def far_block(i):
        back_send[rows_of(i, piece), :] = project_back(planes + i).astype(LOW)

    def near_block(i):
        back_near[rows_of(i, piece), :] = project_back(i)

    each(planes, far_block)
    back_copy = remote(back_send, back_got, sem_back.at[0], sem_back.at[1], partner)
    back_copy.start()
    each(planes, near_block)
    qkv_part[:, :, :near_cols] = qkv_acc[...].astype(LOW).reshape(groups, dense_rows, near_cols)
    turned = jnp.broadcast_to(first_acc[...], (LANES, width)).T.astype(LOW)
    qkv_part[:, :, near_cols:] = turned.reshape(groups, dense_rows, LANES)

    def qkv_copy(i):
        return give(qkv_part.at[i], qkv_got, sem_qkv, i)

    others(lambda i: qkv_copy(i).start())

    back_copy.wait_recv()

    def finish(b):
        r = rows_of(b, piece)
        scaled, inverse = normalize(x[b].astype(F32))
        grad = back_near[r, :] + back_got[r, :].astype(F32)
        first = norm_backward(grad, scaled, inverse, first_gain)
        up[b] = (res_grad[r, :] + first).astype(LOW)
        in_start(b)

    each(planes, finish)

    others(lambda i: taken(rest_part.at[i], rest_got, sem_rest, i).wait_recv())
    others(lambda i: taken(qkv_part.at[i], qkv_got, sem_qkv, i).wait_recv())

    def from_group(mine_part, got, i):
        return jnp.where(i == me, mine_part[i], got[i]).astype(F32)

    def add(j, sums_of):
        first, second, rest = sums_of
        first += from_group(qkv_part, qkv_got, 2 * j)
        second += from_group(qkv_part, qkv_got, 2 * j + 1)
        rest += from_group(rest_part, rest_got, 2 * j)
        rest += from_group(rest_part, rest_got, 2 * j + 1)
        return first, second, rest

    zero = jnp.zeros(qkv_part.shape[1:], F32)
    first, second, rest = lax.fori_loop(
        0, groups // 2, add, (zero, zero, jnp.zeros(rest_part.shape[1:], F32))
    )
    columns = []
    for kind in kinds:
        for side in (first, second):
            columns.append(side[:, kind * near_width : (kind + 1) * near_width])
    columns += [rest, first[:, near_cols:] + second[:, near_cols:]]
    share = jnp.concatenate(columns, axis=1).astype(LOW)
    cut = dense_rows // planes
    for z in range(planes):
        part[z] = share[z * cut : (z + 1) * cut]

    def over_planes(body):
        each(planes - 1, lambda i: body(lax.rem(place + 1 + i, planes)))

    def tell_part(z):
        return remote(part.at[z], heard.at[place], sem_part.at[0, z], sem_part.at[1, place], (me, z))

    def hear_part(z):
        return remote(part.at[z], heard.at[z], sem_part.at[0, z], sem_part.at[1, z], (me, z))

    def tell_sum(z):
        target = total_out.at[place]
        return remote(summed, target, sem_total.at[0, z], sem_total.at[1, place], (me, z))

    def hear_sum(z):
        return remote(summed, total_out.at[z], sem_total.at[0, z], sem_total.at[1, z], (me, z))

    over_planes(lambda z: tell_part(z).start())
    over_planes(lambda z: hear_part(z).wait_recv())
    sum_of = part[place].astype(F32)
    for k in range(1, planes):
        sum_of += heard[lax.rem(place + k, planes)].astype(F32)
    summed[...] = sum_of.astype(LOW)
    over_planes(lambda z: tell_sum(z).start())
    put = copy_here(summed, total_out.at[place])
    put.start()

    x_finish()
    seg_finish()

    def end_dense(i):
        give(task_part, task_all, sem_task, i).wait_send()
        give(tiny_in, tiny_all, sem_tiny, i).wait_send()
        give(attn_in, attn_all, sem_attn, i).wait_send()
        for kind in kinds:
            near_copy(i, kind, i, me).wait_send()
        rest_copy(i).wait_send()
        qkv_copy(i).wait_send()

    others(end_dense)
    save_sel.wait()
    for p in range(pairs):
        att_copy(p).wait_send()
        att_back_copy(p).wait_send()
    back_copy.wait_send()
    for c in range(chunks):
        ga_sent(c)
        ga_received(c)
        gb_sent(c)
        for kind in range(2):
            phase_copy(kind, c).wait_send()
            sums_copy(kind, c).wait()
    over_planes(lambda z: tell_part(z).wait_send())
    over_planes(lambda z: tell_sum(z).wait_send())
    over_planes(lambda z: hear_sum(z).wait_recv())
    put.wait()
    out_end()
    in_end()


def greet_all(groups, planes):
    me = lax.axis_index("dp")
    place = lax.axis_index("seq")
    base = me - lax.rem(me, 2)
    band = 2 * (place // 2)
    mine = me * 2 + lax.rem(place, 2)
    barrier = pltpu.get_barrier_semaphore()

    def signal(dp, z):
        pl.semaphore_signal(barrier, inc=1, device_id=(dp, z), device_id_type=MESH)

    def near_planes(i):
        m = lax.rem(mine + 1 + i, 2 * groups)
        signal(m // 2, band + lax.rem(m, 2))

    each(2 * groups - 1, near_planes)
    each(4, lambda i: signal(base + i // 2, 2 - band + lax.rem(i, 2)))
    pl.semaphore_wait(barrier, 2 * groups + 3)


def layer(te, acts, seg, up_in, qkv, attn, tiny, task, win, wout, groups, planes, experts):
    _, piece, width = acts.shape
    half = planes * piece
    tokens = 2 * half
    heads = width // HEAD // 2
    pairs = heads // 2
    hidden = win.shape[0] // experts
    chunks = 4 if hidden % 64 == 0 else 1
    rows = hidden // chunks
    count = 2 * groups
    dense_rows = qkv.shape[0]
    near_cols = 3 * heads * HEAD
    anywhere = pl.BlockSpec(memory_space=pl.ANY)
    dma = pltpu.SemaphoreType.DMA
    S = lambda shape, t=LOW: jax.ShapeDtypeStruct(shape, t)
    V = lambda shape, t=LOW: pltpu.VMEM(shape, t)
    pieces = (planes, piece, width)
    head_shape = (heads, tokens, LANES)
    pair_shape = (pairs, tokens, LANES)
    band_shape = (chunks, count, 2, rows, width)
    both_shape = (max(half, 2 * win.shape[0]), width)
    sel_shape = (count, rows, rows * experts)
    rest_shape = (groups, dense_rows, width + LANES)
    qkv_shape = (groups, dense_rows, near_cols + LANES)
    total = (planes, dense_rows // planes, 4 * width + 2 * LANES)
    return pl.pallas_call(
        functools.partial(layer_kernel, groups, planes, experts),
        in_specs=[pl.BlockSpec(memory_space=pltpu.SMEM)] + [anywhere] * 9,
        out_specs=[anywhere] * 7,
        out_shape=[
            S(pieces),
            S(pieces),
            S(total),
            S(both_shape),
            S(band_shape),
            S(band_shape),
            S(sel_shape),
        ],
        scratch_shapes=[
            V((2 * planes, piece, width)),
            V((2 * planes, 2, piece), jnp.int32),
            V((2 * planes, piece, width)),
            V(pieces, F32),
            V(pieces),
            V(both_shape),
            V(both_shape),
            V((groups, dense_rows, near_cols)),
            V((groups, dense_rows, width)),
            V((groups,) + tiny.shape),
            V((width, LANES), F32),
            V(sel_shape),
            V((groups, 2, LANES), jnp.int32),
            pltpu.SMEM((groups, 2, LANES), jnp.int32),
            V(head_shape),
            V(head_shape),
            V(head_shape),
            V(pair_shape),
            V(pair_shape),
            V((tokens, width)),
            V((tokens, LANES), F32),
            V((tokens, width)),
            V((tokens, heads * HEAD)),
            V(band_shape),
            V(band_shape),
            V(band_shape),
            V((tokens, width), F32),
            V((tokens, width), F32),
            V((half, width)),
            V((half, width)),
            V((half, LANES), F32),
            V(pair_shape),
            V((pairs, half, LANES)),
            V((width, width), F32),
            V((width, LANES), F32),
            V((1, width), F32),
            V(rest_shape),
            V(rest_shape),
            V((tokens, LANES)),
            V((HEAD, tokens)),
            V((HEAD, tokens), F32),
            V((width, near_cols), F32),
            V((1, width), F32),
            V(qkv_shape),
            V(qkv_shape),
            V(total),
            V(total),
            V(total[1:]),
            V(both_shape),
        ]
        + [dma((2, planes))] * 6
        + [dma((2, groups, 3))]
        + [dma((2, groups))] * 3
        + [dma((2, 2, chunks)), dma((1, 2, count))]
        + [dma((chunks, 2, count))] * 3
        + [dma((2, pairs)), dma((2, 3)), dma((2, 2, chunks)), dma((2, planes)), dma((2, pairs))]
        + [dma((2, groups)), dma((2,)), dma((2, groups))]
        + [dma((2, planes))] * 3
        + [dma((5, chunks)), dma((32,))],
        compiler_params=pltpu.CompilerParams(
            collective_id=0, has_side_effects=True, vmem_limit_bytes=LARGE
        ),
        cost_estimate=cost(250),
        name="layer",
    )(te, acts, seg, up_in, qkv, attn, tiny, task, win, wout)


def deliver_kernel(
    sel, ga, other, tokens, grads, total,
    outputs, input_grad, qkv_grad, attn_grad, router_grad, first, second, win_grad, wout_grad,
):
    outputs[...] = tokens[...]
    input_grad[...] = grads[...].astype(F32)
    count, rows, columns = sel.shape
    width = ga.shape[4]
    choice = sel[...].reshape(count * rows, columns)
    for kind, grad in ((0, win_grad), (1, wout_grad)):
        values = dot_tn(choice, ga[0, :, kind].reshape(count * rows, width))
        grad[...] = values + other[kind].astype(F32)

    @pl.when(pl.program_id(0) == 0)
    def _():
        planes, cut, _ = total.shape
        for z in range(planes):
            r = slice(z * cut, (z + 1) * cut)
            values = total[z].astype(F32)
            qkv_grad[r] = values[:, : 3 * width]
            attn_grad[r] = values[:, 3 * width : 4 * width]
        small = jnp.concatenate([total[z, :, 4 * width :].astype(F32) for z in range(planes)])
        turned = small[:, :LANES].T
        router_grad[...] = turned[: router_grad.shape[0]]
        second[...] = turned[EXPERTS_AT : EXPERTS_AT + 1]
        first[...] = small[:, LANES:].T[0:1]


def deliver(sel, ga, other, tokens, grads, total, experts):
    chunks = ga.shape[0]
    planes, piece, width = tokens.shape
    dense_rows = total.shape[0] * total.shape[1]
    part = pl.BlockSpec((planes // chunks, piece, width), lambda i: (i, 0, 0))
    rows = other.shape[1] // chunks
    grad = pl.BlockSpec((rows, width), lambda i: (i, 0))
    S = lambda shape, t=F32: jax.ShapeDtypeStruct(shape, t)
    return pl.pallas_call(
        deliver_kernel,
        grid=(chunks,),
        in_specs=[
            whole(*sel.shape),
            pl.BlockSpec((1,) + ga.shape[1:], lambda i: (i, 0, 0, 0, 0)),
            pl.BlockSpec((2, rows, width), lambda i: (0, i, 0)),
            part,
            part,
            whole(*total.shape),
        ],
        out_specs=[
            part,
            part,
            whole(dense_rows, 3 * width),
            whole(dense_rows, width),
            whole(experts, dense_rows),
            whole(1, dense_rows),
            whole(1, dense_rows),
            grad,
            grad,
        ],
        out_shape=[
            S(tokens.shape, LOW),
            S(tokens.shape),
            S((dense_rows, 3 * width)),
            S((dense_rows, width)),
            S((experts, dense_rows)),
            S((1, dense_rows)),
            S((1, dense_rows)),
            S(other.shape[1:]),
            S(other.shape[1:]),
        ],
        compiler_params=pltpu.CompilerParams(vmem_limit_bytes=LARGE),
        cost_estimate=cost(5),
        name="deliver",
    )(sel, ga, other, tokens, grads, total)


def local(
    activations, qkv_weight, attn_weight, router_weight, gain_one, gain_two,
    expert_in, expert_out, segments, task_ids, task_experts, out_grad,
):
    packs, length, width = activations.shape
    planes = lax.axis_size("seq")
    groups = lax.axis_size("dp")
    cuts = 2 * packs
    assert cuts == planes == 4 and groups % 2 == 0
    piece = length // 2
    experts = router_weight.shape[1]
    hidden = expert_in.shape[0]
    assert experts + 2 <= TINY
    zeros = jnp.zeros((TINY - experts - 2, qkv_weight.shape[0]), LOW)
    tiny = jnp.concatenate([router_weight.T, gain_one[None], gain_two[None], zeros])
    tokens, grads, total, other, expert_grads, _, sel = layer(
        task_experts.T,
        activations.reshape(cuts, piece, width),
        segments,
        out_grad.reshape(cuts, piece, width),
        qkv_weight,
        attn_weight,
        tiny,
        task_ids,
        expert_in.reshape(hidden * experts, width),
        expert_out.reshape(hidden * experts, width),
        groups,
        planes,
        experts,
    )
    outputs, input_grad, qkv_grad, attn_grad, router_grad, first, second, win_grad, wout_grad = (
        deliver(
            sel,
            expert_grads,
            other.reshape(2, -1, width)[:, : hidden * experts],
            tokens,
            grads,
            total,
            experts,
        )
    )
    return (
        outputs.reshape(packs, length, width),
        input_grad.reshape(packs, length, width),
        qkv_grad,
        attn_grad,
        router_grad.T,
        first.reshape(-1),
        second.reshape(-1),
        win_grad.reshape(expert_in.shape),
        wout_grad.reshape(expert_in.shape),
    )


def solution(mesh):
    placed = (
        P("dp", "seq", None),
        P("dp", None),
        P("dp", None),
        P("dp", None),
        P("dp"),
        P("dp"),
        P(("dp", "seq"), None, None),
        P(("dp", "seq"), None, None),
        P("dp", "seq"),
        P("dp", "seq"),
        P(),
        P("dp", "seq", None),
    )
    return jax.shard_map(
        local,
        mesh=mesh,
        in_specs=placed,
        out_specs=(
            P("dp", "seq", None),
            P("dp", "seq", None),
            P("dp", None),
            P("dp", None),
            P("dp", None),
            P("dp"),
            P("dp"),
            P(("dp", "seq"), None, None),
            P(("dp", "seq"), None, None),
        ),
        check_vma=False,
    )
```

profile of v0, /device:TPU:0, one launch (start us, length us, event | category | flops | bytes accessed | tf_op | source)
XLA Modules:
  0.0 264.9 jit_solution(9452184151449183142)
XLA Ops:
  0.7 0.1 pad.3.clone
  0.7 1.4 maximum_maximum_fusion.tiny_in
  2.1 256.5 %layer.1 = (bf16[4,256,512]{2,1,0:T(8,128)(2,1)}, bf16[4,256,512]{2,1,0:T(8,128)(2,1)}, bf16[4,16,2304]{2,1,0:T(8,128)(2,1)}, bf16[1024,512]{1,0:T(8,128)(2,1)},...) custom-call(s32[2,16]{1,0:T(2,128)} %bitcast.29, ...), custom_call_target="tpu_custom_call" | custom-call | flops 2500000000 | bytes 1024 | tf_op jit(solution)/shard_map/layer/pallas_call | solution.py:910
  258.6 6.0 %deliver.1 = (bf16[4,256,512]{2,1,0:T(8,128)(2,1)}, f32[4,256,512]{2,1,0:T(8,128)}, f32[64,1536]{1,0:T(8,128)}, f32[64,512]{1,0:T(8,128)}, f32[8,64]{1,0:T(8,128...) custom-call(bf16[16,16,128]{2,1,0:T(8,128)(2,1)} %get-tuple-element.24.sel, ...), custom_call_target="tpu_custom_call" | custom-call | flops 50000000 | bytes 1024 | tf_op jit(solution)/shard_map/deliver/pallas_call | solution.py:1027
  (1 shorter events, 0.0 us)
where the time goes:
time: 269 us; the launch traced here: 265 us
  Pallas kernels  262 us (97%)
    pallas_call x1, Pallas kernels, layer(): pl.pallas_call(functools.partial(layer_kernel, groups, planes, experts),...  256 us
    pallas_call x1, Pallas kernels, deliver(): pl.pallas_call(deliver_kernel, grid=(chunks,), in_specs=[whole(*sel.shape...  6 us

commit v1 on v0

--- a/solution.py
+++ b/solution.py
@@ -98,7 +98,7 @@
 
 def layer_kernel(
     groups, planes, experts, te, acts, seg, up_in, qkv_in, attn_in, tiny_in, task, win_in, wout_in,
-    tokens_out, grads_out, total_out, other_got, ga_got, gb_got, sel_out,
+    tokens_out, grads_out, total_out, other_got, ga_got, gb_got, far_w, sel_out,
     x, segx, up, res, stage, both, other, near_all, attn_all, tiny_all, small, sel, task_all, task_s,
     qa, ka, va, att, attf, normed, gates, slot, dv, send, got_a, got_b, out, dx, far_value, far_dx,
     far_gate, att_grad, att_send, attn_acc, router_acc, gain_acc, rest_part, rest_got, gb, key_t,
@@ -112,14 +112,16 @@
     core = lax.rem(me, 2)
     base = me - core
     partner = (base + 1 - core, place)
-    peer = (me, place + 2 - 4 * (place // 2))
     band = 2 * (place // 2)
+    hub = 1 + place // 2
+    at_hub = place == hub
     mine = me * 2 + lax.rem(place, 2)
     count = 2 * groups
     piece, width = x.shape[1], x.shape[2]
     tokens = 2 * planes * piece
     half = tokens // 2
-    chunks, _, _, rows, _ = send.shape
+    slots = send.shape[0]
+    chunks, _, _, rows, _ = got_a.shape
     chunk_rows = rows * experts
     heads = qa.shape[0]
     pairs = heads // 2
@@ -272,14 +274,47 @@
         return pl.ds(at if isinstance(c, int) else pl.multiple_of(at, chunk_rows), chunk_rows)
 
     def phase_copy(kind, c):
-        source = (win_in, wout_in)[kind].at[rows_of(c, chunk_rows)]
-        target = other.at[part_of(kind, c)]
-        return remote(source, target, sem_phase.at[0, kind, c], sem_phase.at[1, kind, c], peer)
-
-    def sums_copy(kind, c):
+        r = rows_of(c, chunk_rows)
+        return remote(
+            (win_in, wout_in)[kind].at[r],
+            far_w.at[lax.rem(place, 2), kind, r],
+            sem_phase.at[0, 0, kind, c],
+            sem_phase.at[1, lax.rem(place, 2), kind, c],
+            (me, 3 - hub),
+        )
+
+    def phase_got(b, kind, c):
+        r = rows_of(c, chunk_rows)
+        return remote(
+            (win_in, wout_in)[kind].at[r],
+            far_w.at[b, kind, r],
+            sem_phase.at[0, 0, kind, c],
+            sem_phase.at[1, b, kind, c],
+            (me, 2 - band + b),
+        )
+
+    def ring(c, b):
+        at = lax.rem(2 * c + b, 4) * 2 * chunk_rows
+        return at if isinstance(at, int) else pl.multiple_of(at, chunk_rows)
+
+    def sums_copy(kind, c, b):
+        r = pl.ds(ring(c, b) + kind * chunk_rows, chunk_rows)
+        return remote(
+            sums.at[r],
+            other_got.at[part_of(kind, c)],
+            sem_sums.at[0, b, kind, c],
+            sem_sums.at[1, 0, kind, c],
+            (me, 2 - band + b),
+        )
+
+    def sums_got(kind, c):
         r = part_of(kind, c)
         return remote(
-            sums.at[r], other_got.at[r], sem_sums.at[0, kind, c], sem_sums.at[1, kind, c], peer
+            sums.at[pl.ds(0, chunk_rows)],
+            other_got.at[r],
+            sem_sums.at[0, 0, kind, c],
+            sem_sums.at[1, 0, kind, c],
+            (me, 3 - hub),
         )
 
     def band_device(m):
@@ -319,14 +354,107 @@
         )
 
     a_start, a_sent, a_received = band_copies(
-        lambda c, m: send.at[:, m], lambda c, m: got_a.at[:, m], sem_a, home.at[0]
+        lambda c, m: send.at[pl.ds(0, chunks), m], lambda c, m: got_a.at[:, m], sem_a, home.at[3]
     )
-    b_start, b_sent, b_received = by_chunk(send, got_b, sem_b, home.at[1])
-    ga_start, ga_sent, ga_received = by_chunk(got_a, ga_got, sem_ga, home.at[2])
-    gb_start, gb_sent, gb_received = by_chunk(got_b, gb_got, sem_gb, home.at[3])
-
-    def load_gb(c):
-        return pltpu.make_async_copy(gb_got.at[c], send.at[c], home.at[4, c])
+    ga_start, ga_sent, ga_received = by_chunk(got_a, ga_got, sem_ga, home.at[0])
+
+    def far_rows(dp):
+        return pl.ds(2 * dp, 2)
+
+    def b_slots(c):
+        return pl.ds(lax.rem(2 * c, slots), 2)
+
+    def b_part(c, m):
+        return remote(
+            send.at[b_slots(c), m],
+            got_b.at[c, far_rows(me)],
+            sem_b.at[c, 0, m],
+            sem_b.at[c, 1, me],
+            band_device(m),
+        )
+
+    def b_home(c):
+        return pltpu.make_async_copy(
+            send.at[b_slots(c), mine], got_b.at[c, far_rows(me)], home.at[1, c]
+        )
+
+    def others_of_band(body):
+        each(count - 1, lambda i: body(lax.rem(mine + 1 + i, count)))
+
+    def b_start(c):
+        b_home(c).start()
+        others_of_band(lambda m: b_part(c, m).start())
+        b_home(c).wait()
+
+    def b_sent(c):
+        others_of_band(lambda m: b_part(c, m).wait_send())
+
+    def b_received(c):
+        def one(dp):
+            @pl.when(jnp.logical_not(at_hub & (dp == me)))
+            def _():
+                remote(
+                    send.at[pl.ds(0, 2), 0],
+                    got_b.at[c, far_rows(dp)],
+                    sem_b.at[c, 0, dp],
+                    sem_b.at[c, 1, dp],
+                    (dp, hub),
+                ).wait_recv()
+
+        each(groups, one)
+
+    def gb_part(c, dp):
+        return remote(
+            got_b.at[c, far_rows(dp)],
+            gb_got.at[c, :, :, rows_of(mine, rows)],
+            sem_gb.at[c, 0, dp],
+            sem_gb.at[c, 1, mine],
+            (dp, hub),
+        )
+
+    def gb_home(c):
+        target = gb_got.at[c, :, :, rows_of(mine, rows)]
+        return pltpu.make_async_copy(got_b.at[c, far_rows(me)], target, home.at[2, c])
+
+    def gb_each(body):
+        def one(j):
+            dp = lax.rem(me + 1 + j, groups)
+
+            @pl.when(jnp.logical_not(at_hub & (dp == me)))
+            def _():
+                body(dp)
+
+        each(groups, one)
+
+    def gb_start(c):
+        gb_each(lambda dp: gb_part(c, dp).start())
+
+        @pl.when(at_hub)
+        def _():
+            gb_home(c).start()
+
+    def gb_sent(c):
+        gb_each(lambda dp: gb_part(c, dp).wait_send())
+
+    def gb_received(c):
+        others_of_band(
+            lambda m: remote(
+                got_b.at[c, pl.ds(0, 2)],
+                gb_got.at[c, :, :, rows_of(m, rows)],
+                sem_gb.at[c, 0, 0],
+                sem_gb.at[c, 1, m],
+                band_device(m),
+            ).wait_recv()
+        )
+        gb_home(c).wait()
+
+    def staged(b, kind, size):
+        at = (2 * b + kind) * size
+        return pl.ds(at if 4 * size <= other.shape[0] else 0, size)
+
+    def load_gb(c, b, kind):
+        target = other.at[staged(b, kind, count * rows)]
+        return pltpu.make_async_copy(gb_got.at[c, b, kind], target, home.at[5 + b, kind])
 
     x_start()
     seg_start()
@@ -376,16 +504,15 @@
     save_sel = copy_here(sel, sel_out)
     save_sel.start()
 
-    def choose(source, c):
+    def choose(source, target):
         choice = sel[...].reshape(count * rows, chunk_rows)
         for kind in range(2):
-            values = dot(choice, source[part_of(kind, c), :])
-            send[c, :, kind] = values.astype(LOW).reshape(count, rows, width)
+            values = dot(choice, source(kind))
+            target[:, kind] = values.astype(LOW).reshape(count, rows, width)
 
     for copy in load_both:
         copy.wait()
-    for c in range(chunks):
-        choose(both, c)
+    each(chunks, lambda c: choose(lambda kind: both[part_of(kind, c), :], send.at[c]))
 
     def end_near(i):
         for kind in kinds:
@@ -446,23 +573,29 @@
         for kind in range(2):
             phase_copy(kind, c).start()
 
-    for k in range(planes):
-        arrive(by_distance(k))
-        if k < planes // 2:
-            project(by_distance(k))
-    up_start()
-    a_start(0)
-    start_phase(0)
-    others(lambda i: give(attn_in, attn_all, sem_attn, i).start())
-    for k in range(planes // 2, planes):
-        project(by_distance(k))
-
     def far_piece(k):
         x_far(k)
         seg_far(k)
         project(planes + k)
 
-    each(planes, far_piece)
+    near_order = [by_distance(k) for k in range(planes)]
+    arrive(near_order[0])
+    project(near_order[0])
+    arrive(near_order[1])
+    project(near_order[1])
+    far_piece(near_order[0])
+    for k in near_order[2:]:
+        arrive(k)
+    up_start()
+    a_start(0)
+    for c in range(min(2, chunks)):
+        start_phase(c)
+    others(lambda i: give(attn_in, attn_all, sem_attn, i).start())
+    far_piece(near_order[1])
+    for k in near_order[2:]:
+        project(k)
+    for k in near_order[2:]:
+        far_piece(k)
 
     block = min(512, half)
 
@@ -488,17 +621,35 @@
 
         each(tokens // block, attend)
         att_copy(p).start()
-        if p == 0 and chunks > 1:
-            start_phase(1)
+        if p == 0:
+            for c in range(2, chunks):
+                start_phase(c)
 
     def other_weights(c):
-        for kind in range(2):
-            phase_copy(kind, c).wait_recv()
-        choose(other, c)
-        b_start(c)
-
-    for c in range(2, chunks):
-        start_phase(c)
+        @pl.when(at_hub)
+        def _():
+            loads = []
+            for b in range(2):
+                for kind in range(2):
+                    phase_got(b, kind, c).wait_recv()
+                    source = far_w.at[b, kind, rows_of(c, chunk_rows)]
+                    target = other.at[staged(b, kind, chunk_rows)]
+                    loads.append(pltpu.make_async_copy(source, target, home.at[7 + b, kind]))
+                    loads[-1].start()
+
+            @pl.when(2 * c >= slots)
+            def _():
+                b_sent(c - slots // 2)
+
+            for b in range(2):
+                for kind in range(2):
+                    loads[2 * b + kind].wait()
+                choose(
+                    lambda kind: other[staged(b, kind, chunk_rows), :],
+                    send.at[lax.rem(2 * c, slots) + b],
+                )
+            b_start(c)
+
     for k in range(planes):
         up_receive(by_distance(k))
     for p in range(pairs):
@@ -542,15 +693,30 @@
     each(2 * planes, middle)
 
     def add_up_others(c):
-        b_sent(c)
-        gb_received(c)
-        load_gb(c).start()
-        load_gb(c).wait()
-        choice = sel[...].reshape(count * rows, chunk_rows)
-        for kind in range(2):
-            values = send[c, :, kind].reshape(count * rows, width)
-            sums[part_of(kind, c), :] = dot_tn(choice, values).astype(LOW)
-            sums_copy(kind, c).start()
+        @pl.when(at_hub)
+        def _():
+            together = 4 * count * rows <= other.shape[0]
+            choice = sel[...].reshape(count * rows, chunk_rows)
+            gb_received(c)
+            if together:
+                for b in range(2):
+                    for kind in range(2):
+                        load_gb(c, b, kind).start()
+            for b in range(2):
+
+                @pl.when(2 * c + b >= 4)
+                def _():
+                    for kind in range(2):
+                        sums_copy(kind, c - 2, b).wait_send()
+
+                for kind in range(2):
+                    if not together:
+                        load_gb(c, b, kind).start()
+                    load_gb(c, b, kind).wait()
+                    r = pl.ds(ring(c, b) + kind * chunk_rows, chunk_rows)
+                    values = other[staged(b, kind, count * rows), :]
+                    sums[r, :] = dot_tn(choice, values).astype(LOW)
+                    sums_copy(kind, c, b).start()
 
     out[...] = jnp.zeros_like(out)
     dx[...] = jnp.zeros_like(dx)
@@ -574,32 +740,37 @@
 
         each(count // per, tile)
 
-    def second(c):
-        b_received(c)
-        expert(got_b, c)
-        gb_start(c)
-
     a_sent(0)
     a_received(0)
-    if chunks > 1:
-        other_weights(0)
-        expert(got_a, 0)
-        other_weights(1)
-        expert(got_a, 1)
-        second(0)
-        other_weights(2)
-        expert(got_a, 2)
-        second(1)
-        other_weights(3)
-        expert(got_a, 3)
-        add_up_others(0)
-        second(2)
-        add_up_others(1)
-        second(3)
-    else:
-        expert(got_a, 0)
-        other_weights(0)
-        second(0)
+    other_weights(0)
+
+    def step_of(j):
+        @pl.when(j < chunks)
+        def _():
+            expert(got_a, j)
+
+        @pl.when(j + 1 < chunks)
+        def _():
+            other_weights(j + 1)
+
+        @pl.when(j > 0)
+        def _():
+            b_received(j - 1)
+            expert(got_b, j - 1)
+            gb_start(j - 1)
+
+        if chunks > 1:
+
+            @pl.when(j == chunks)
+            def _():
+                add_up_others(0)
+
+    each(chunks + 1, step_of)
+
+    @pl.when(at_hub)
+    def _():
+        for c in range(chunks - slots // 2, chunks):
+            b_sent(c)
 
     step = half // 2
     step_lane = lanes_of((step, LANES))
@@ -625,13 +796,14 @@
     for copy in far_copies:
         copy.start()
     up_finish()
-
     res_grad = out.at[pl.ds(half, half)]
     attn_acc[...] = jnp.zeros_like(attn_acc)
     router_acc[...] = jnp.zeros_like(router_acc)
     gain_acc[...] = jnp.zeros_like(gain_acc)
     for copy in far_copies:
         copy.wait()
+    if chunks > 1:
+        add_up_others(1)
 
 
     def post(b):
@@ -691,8 +863,8 @@
 
     others(lambda i: rest_copy(i).start())
 
-    if chunks > 1:
-        add_up_others(2)
+    for c in range(2, chunks - 1):
+        add_up_others(c)
 
     all_lane = lanes_of((tokens, LANES))
     for p in range(pairs):
@@ -853,7 +1025,14 @@
         gb_sent(c)
         for kind in range(2):
             phase_copy(kind, c).wait_send()
-            sums_copy(kind, c).wait()
+            sums_got(kind, c).wait_recv()
+
+    @pl.when(at_hub)
+    def _():
+        for k in range(max(0, 2 * chunks - 4), 2 * chunks):
+            for kind in range(2):
+                sums_copy(kind, k // 2, k % 2).wait_send()
+
     over_planes(lambda z: tell_part(z).wait_send())
     over_planes(lambda z: tell_sum(z).wait_send())
     over_planes(lambda z: hear_sum(z).wait_recv())
@@ -910,14 +1089,15 @@
     return pl.pallas_call(
         functools.partial(layer_kernel, groups, planes, experts),
         in_specs=[pl.BlockSpec(memory_space=pltpu.SMEM)] + [anywhere] * 9,
-        out_specs=[anywhere] * 7,
+        out_specs=[anywhere] * 8,
         out_shape=[
             S(pieces),
             S(pieces),
             S(total),
             S(both_shape),
             S(band_shape),
-            S(band_shape),
+            S((chunks, 2, 2, count * rows, width)),
+            S((2, 2) + win.shape),
             S(sel_shape),
         ],
         scratch_shapes=[
@@ -944,7 +1124,7 @@
             V((tokens, LANES), F32),
             V((tokens, width)),
             V((tokens, heads * HEAD)),
-            V(band_shape),
+            V((max(2, chunks),) + band_shape[1:]),
             V(band_shape),
             V(band_shape),
             V((tokens, width), F32),
@@ -974,12 +1154,12 @@
         + [dma((2, planes))] * 6
         + [dma((2, groups, 3))]
         + [dma((2, groups))] * 3
-        + [dma((2, 2, chunks)), dma((1, 2, count))]
+        + [dma((2, 2, 2, chunks)), dma((1, 2, count))]
         + [dma((chunks, 2, count))] * 3
-        + [dma((2, pairs)), dma((2, 3)), dma((2, 2, chunks)), dma((2, planes)), dma((2, pairs))]
+        + [dma((2, pairs)), dma((2, 3)), dma((2, 2, 2, chunks)), dma((2, planes)), dma((2, pairs))]
         + [dma((2, groups)), dma((2,)), dma((2, groups))]
         + [dma((2, planes))] * 3
-        + [dma((5, chunks)), dma((32,))],
+        + [dma((9, max(2, chunks))), dma((32,))],
         compiler_params=pltpu.CompilerParams(
             collective_id=0, has_side_effects=True, vmem_limit_bytes=LARGE
         ),
@@ -998,8 +1178,10 @@
     width = ga.shape[4]
     choice = sel[...].reshape(count * rows, columns)
     for kind, grad in ((0, win_grad), (1, wout_grad)):
-        values = dot_tn(choice, ga[0, :, kind].reshape(count * rows, width))
-        grad[...] = values + other[kind].astype(F32)
+        for c in range(ga.shape[0]):
+            r = slice(c * columns, (c + 1) * columns)
+            values = dot_tn(choice, ga[c, :, kind].reshape(count * rows, width))
+            grad[r] = values + other[kind, r].astype(F32)
 
     @pl.when(pl.program_id(0) == 0)
     def _():
@@ -1018,18 +1200,20 @@
 
 def deliver(sel, ga, other, tokens, grads, total, experts):
     chunks = ga.shape[0]
+    steps = min(2, chunks)
+    per = chunks // steps
     planes, piece, width = tokens.shape
     dense_rows = total.shape[0] * total.shape[1]
-    part = pl.BlockSpec((planes // chunks, piece, width), lambda i: (i, 0, 0))
-    rows = other.shape[1] // chunks
+    part = pl.BlockSpec((planes // steps, piece, width), lambda i: (i, 0, 0))
+    rows = other.shape[1] // steps
     grad = pl.BlockSpec((rows, width), lambda i: (i, 0))
     S = lambda shape, t=F32: jax.ShapeDtypeStruct(shape, t)
     return pl.pallas_call(
         deliver_kernel,
-        grid=(chunks,),
+        grid=(steps,),
         in_specs=[
             whole(*sel.shape),
-            pl.BlockSpec((1,) + ga.shape[1:], lambda i: (i, 0, 0, 0, 0)),
+            pl.BlockSpec((per,) + ga.shape[1:], lambda i: (i, 0, 0, 0, 0)),
             pl.BlockSpec((2, rows, width), lambda i: (0, i, 0)),
             part,
             part,
@@ -1078,7 +1262,7 @@
     assert experts + 2 <= TINY
     zeros = jnp.zeros((TINY - experts - 2, qkv_weight.shape[0]), LOW)
     tiny = jnp.concatenate([router_weight.T, gain_one[None], gain_two[None], zeros])
-    tokens, grads, total, other, expert_grads, _, sel = layer(
+    tokens, grads, total, other, expert_grads, _, _, sel = layer(
         task_experts.T,
         activations.reshape(cuts, piece, width),
         segments,

time: 269 us -> 260 us (0.967)
  Pallas kernels: 262 us -> 255 us
    pallas_call x1, Pallas kernels: 256 us -> 250 us  [layer(): pl.pallas_call(functools.partial(layer_kernel, groups, planes, experts),...]
where the time goes in v1:
time: 260 us; the launch traced here: 257 us
  Pallas kernels  255 us (98%)
    pallas_call x1, Pallas kernels, layer(): pl.pallas_call(functools.partial(layer_kernel, groups, planes, experts),...  250 us

profile of v1, /device:TPU:0, one launch (start us, length us, event | category | flops | bytes accessed | tf_op | source)
XLA Modules:
  0.0 257.2 jit_solution(11971586618836229143)
XLA Ops:
  0.7 0.1 pad.3.clone
  0.7 1.4 maximum_maximum_fusion.tiny_in
  2.1 250.0 %layer.1 = (bf16[4,256,512]{2,1,0:T(8,128)(2,1)}, bf16[4,256,512]{2,1,0:T(8,128)(2,1)}, bf16[4,16,2304]{2,1,0:T(8,128)(2,1)}, bf16[1024,512]{1,0:T(8,128)(2,1)},...) custom-call(s32[2,16]{1,0:T(2,128)} %bitcast.29, ...), custom_call_target="tpu_custom_call" | custom-call | flops 2500000000 | bytes 1024 | tf_op jit(solution)/shard_map/layer/pallas_call | solution.py:1089
  252.1 4.8 %deliver.1 = (bf16[4,256,512]{2,1,0:T(8,128)(2,1)}, f32[4,256,512]{2,1,0:T(8,128)}, f32[64,1536]{1,0:T(8,128)}, f32[64,512]{1,0:T(8,128)}, f32[8,64]{1,0:T(8,128...) custom-call(bf16[16,16,128]{2,1,0:T(8,128)(2,1)} %get-tuple-element.24.sel, ...), custom_call_target="tpu_custom_call" | custom-call | flops 50000000 | bytes 1024 | tf_op jit(solution)/shard_map/deliver/pallas_call | solution.py:1211
  (1 shorter events, 0.0 us)

commit v2 on v1

--- a/solution.py
+++ b/solution.py
@@ -866,6 +866,8 @@
     for c in range(2, chunks - 1):
         add_up_others(c)
 
+    each(chunks, ga_start)
+
     all_lane = lanes_of((tokens, LANES))
     for p in range(pairs):
         att_back_copy(p).wait_recv()
@@ -898,7 +900,6 @@
             halves.append(dq_acc[...].T * HEAD**-0.5)
             if h == 0:
                 add_up_others(chunks - 1)
-                each(chunks, ga_start)
         slot[:, p * LANES : (p + 1) * LANES] = jnp.concatenate(halves, axis=1).astype(LOW)
 
     qkv_acc[...] = jnp.zeros_like(qkv_acc)

time: 260 us -> 259 us (level)
  no operation moved by 1% of the time
where the time goes in v2:
time: 259 us; the launch traced here: 256 us
  Pallas kernels  253 us (98%)
    pallas_call x1, Pallas kernels, layer(): pl.pallas_call(functools.partial(layer_kernel, groups, planes, experts),...  249 us

profile of v2, /device:TPU:0, one launch (start us, length us, event | category | flops | bytes accessed | tf_op | source)
XLA Modules:
  0.0 255.7 jit_solution(5972457299631772793)
XLA Ops:
  0.7 0.1 pad.3.clone
  0.7 1.4 maximum_maximum_fusion.tiny_in
  2.1 248.6 %layer.1 = (bf16[4,256,512]{2,1,0:T(8,128)(2,1)}, bf16[4,256,512]{2,1,0:T(8,128)(2,1)}, bf16[4,16,2304]{2,1,0:T(8,128)(2,1)}, bf16[1024,512]{1,0:T(8,128)(2,1)},...) custom-call(s32[2,16]{1,0:T(2,128)} %bitcast.29, ...), custom_call_target="tpu_custom_call" | custom-call | flops 2500000000 | bytes 1024 | tf_op jit(solution)/shard_map/layer/pallas_call | solution.py:1090
  250.7 4.8 %deliver.1 = (bf16[4,256,512]{2,1,0:T(8,128)(2,1)}, f32[4,256,512]{2,1,0:T(8,128)}, f32[64,1536]{1,0:T(8,128)}, f32[64,512]{1,0:T(8,128)}, f32[8,64]{1,0:T(8,128...) custom-call(bf16[16,16,128]{2,1,0:T(8,128)(2,1)} %get-tuple-element.24.sel, ...), custom_call_target="tpu_custom_call" | custom-call | flops 50000000 | bytes 1024 | tf_op jit(solution)/shard_map/deliver/pallas_call | solution.py:1212
  (1 shorter events, 0.0 us)
